TPU v7x, 32 devices: a whole 2x2x4 slice. The times are simulated.
32 devices in a mesh: groups: 2 (over y), aux: 4 (over z), basis: 2 (over x), occ: 2 (over core).
Axes of the slice: x: 2, y: 2, z: 4, core: 2. Of those that a mesh axis runs over, the one named last changes fastest.
Arguments:
- integrals: bfloat16 [4096, 8, 2048], P(('groups', 'basis'), 'aux', 'occ'), parts along dimension 0, may hold values from -0.5 to 0.5
- need_blocks: int32 [4, 8], P('groups'), parts along dimension 0, may hold values from 0 to 15, as said below
- pair_first: int32 [4, 24], P('groups'), parts along dimension 0, may hold values from 0 to 6, as said below
- pair_second: int32 [4, 24], P('groups'), parts along dimension 0, may hold values from 1 to 7
- pair_count: int32 [4], P('groups'), parts along dimension 0, may hold values from 8 to 24, as said below
Outputs:
- k_tiles: float32 [4, 24, 128, 128], P(('groups', 'basis'), None, ('aux', 'occ')), parts along dimension 0
There are 2 independent parts, one for each index of `groups`. A program takes and returns all parts, laid end to end along the dimension named above; each array names one. Nothing has to cross between parts.
Inputs may be any that keep to these rules, and one draw needn't show every extreme that they name: `need_blocks`: each row lists 8 different blocks in rising order; at most 4 of a row lie in one index of basis's range (blocks b * 8 to (b + 1) * 8 - 1), and exactly 4 in some range in every row. pair_first[k, p] < pair_second[k, p]; the pairs of one owner are different. `pair_count`: some owner has exactly 24 live pairs.
All inputs are finite; a program needn't handle non-finite values.
Results may differ from a plain program's by a relative error of at most 0.0003.
Values may be sent and summed in bfloat16 or wider, within the bound.
A program may use at most 64 MiB of HBM per device.

v0:
```python
import jax
import jax.numpy as jnp
from jax import lax
from jax.sharding import PartitionSpec as P

BLK = 128
PMAX = 24


def shards(integrals, need_blocks, pair_first, pair_second, pair_count):
    rows, aux_size, occ_size = integrals.shape
    blk_dev = rows // BLK
    width = aux_size * occ_size
    owner_id = lax.axis_index("basis")
    wanted = lax.dynamic_index_in_dim(need_blocks, owner_id, 0, keepdims=False)
    local_blocks = integrals.reshape(blk_dev, BLK, width)
    window_blocks = lax.all_gather(local_blocks, "basis", axis=0, tiled=True)
    chosen = jnp.take(window_blocks, wanted, axis=0)
    surviving_count = pair_count[owner_id]
    first_ids = lax.dynamic_index_in_dim(pair_first, owner_id, 0, keepdims=False)
    second_ids = lax.dynamic_index_in_dim(pair_second, owner_id, 0, keepdims=False)
    group_size = 4
    turn_count = (surviving_count + group_size - 1) // group_size

    def single_round(step, partial_tiles):
        slot_indices = step * group_size + jnp.arange(group_size)
        clipped = jnp.minimum(slot_indices, PMAX - 1)
        bra_block_rows = jnp.take(chosen, jnp.take(first_ids, clipped), axis=0)
        ket_block_rows = jnp.take(chosen, jnp.take(second_ids, clipped), axis=0)
        product = jnp.einsum(
            "joh,jih->joi", bra_block_rows, ket_block_rows, preferred_element_type=jnp.float32
        )
        product = jnp.where(
            (slot_indices < surviving_count)[:, None, None], product, jnp.zeros_like(product)
        )
        return lax.dynamic_update_slice_in_dim(partial_tiles, product, step * group_size, 0)

    partial_tiles = lax.fori_loop(
        0, turn_count, single_round, jnp.zeros((PMAX, BLK, BLK), jnp.float32)
    )
    shares = lax.psum_scatter(partial_tiles, ("aux", "occ"), scatter_dimension=1, tiled=True)
    return shares[None]


def solution(mesh):
    in_specs = (
        P(("groups", "basis"), "aux", "occ"),
        P("groups", None),
        P("groups", None),
        P("groups", None),
        P("groups"),
    )
    out_specs = P(("groups", "basis"), None, ("aux", "occ"), None)
    return jax.shard_map(shards, mesh=mesh, in_specs=in_specs, out_specs=out_specs, check_vma=False)
```

profile of v0, /device:TPU:0, one launch (start us, length us, event | category | flops | bytes accessed | tf_op | source)
XLA Modules:
  0.0 247.2 jit_solution(7608950498415389050)
XLA Ops:
  6.5 7.9 %reshape.52 = bf16[8,128,2048]{2,1,0:T(8,128)(2,1)} reshape(bf16[1024,2,1024]{2,1,0:T(2,128)(2,1)} %param.11) | data formatting | bytes 8388608 | tf_op jit(solution)/shard_map/reshape | solution.py:16
  16.3 105.0 %all-gather.2.cloned.1.call-done = bf16[16,128,2048]{2,1,0:T(8,128)(2,1)} async-done(((bf16[8,128,2048]{2,1,0:T(8,128)(2,1)}), bf16[16,128,2048]{2,1,0:T(8,128)(2,1)}) %all-gather.2.cloned.1.call-update) | async-done | bytes 8388624 | tf_op jit(solution)/shard_map/all_gather | solution.py:17
  121.3 6.2 %gather_fusion.4 = bf16[8,128,2048]{2,1,0:T(8,128)(2,1)} fusion(bf16[16,128,2048]{2,1,0:T(8,128)(2,1)} %all-gather.2.cloned.1.call-done, s32[1024]{0:T(1024)S(1)} %pad_clamp_fusion.3), kind=kCustom, calls=%fused_computation.4 | custom fusion | bytes 8388640 | tf_op jit(solution)/shard_map/jit(_take)/gather | solution.py:18
  127.4 4.6 %broadcast_select_fusion = bf16[8,128,2048]{2,1,0:T(8,128)(2,1)} fusion(bf16[8,128,2048]{2,1,0:T(8,128)(2,1)} %gather_fusion.4, pred[8]{0:T(512)(128)(4,1)S(1)} %compare_and_fusion.3), kind=kLoop, calls=%fused_computation.25 | loop fusion | flops 2097152 | bytes 8388616 | tf_op jit(solution)/shard_map/jit(_take)/select_n | solution.py:18
  132.1 1.3 broadcast_in_dim.37
  133.4 72.4 %while.10 = (s32[]{:T(128)}, f32[24,128,128]{2,1,0:T(8,128)}, s32[]{:T(128)}, s32[]{:T(128)}, s32[24]{0:T(128)S(1)}, /*index=5*/bf16[8,128,2048]{2,1,0:T(8,128)(...) while((s32[]{:T(128)}, f32[24,128,128]{2,1,0:T(8,128)}, s32[]{:T(128)}, ...), condition=%wide.region_1.4_spmd, body=%wide.region_0.0_spmd.sunk | while | flops 270601344 | bytes 12857799 | solution.py:38
  133.4 0.6 gather_fusion
  134.1 0.6 gather_fusion.1
  134.7 2.9 %gather_fusion.2 = bf16[4,128,2048]{2,1,0:T(8,128)(2,1)S(1)} fusion(bf16[8,128,2048]{2,1,0:T(8,128)(2,1)} %get-tuple-element.147, s32[1024]{0:T(1024)S(1)} %pad_clamp_fusion.8), kind=kCustom, calls=%fused_computation.3.clone.clone.1 | custom fusion | bytes 4194320 | tf_op jit(solution)/shard_map/while/body/jit(_take)/gather | solution.py:29
  137.6 4.2 %gather_fusion.3 = bf16[4,128,2048]{2,1,0:T(8,128)(2,1)} fusion(bf16[8,128,2048]{2,1,0:T(8,128)(2,1)} %get-tuple-element.147, s32[1024]{0:T(1024)S(1)} %pad_clamp_fusion.9), kind=kCustom, calls=%fused_computation.1.clone.clone.1 | custom fusion | bytes 4194320 | tf_op jit(solution)/shard_map/while/body/jit(_take)/gather | solution.py:28
  142.4 3.1 %fusion.28 = f32[24,128,128]{2,1,0:T(8,128)} fusion(f32[24,128,128]{2,1,0:T(8,128)} %get-tuple-element.132, s32[]{:T(128)S(6)} %select_n.118, bf16[4,128,2048]{2,1,0:T(8,128)(2,1)S(1)} %gather_fusion.2, pred[4]{0:T(512)(128)(4,1)S(1)} %get-tuple-element.117, bf16[4,128,2048]{2,1,0:T(8,128)(2,1)} %gather_fusion.3, ...), kind=kOutput, calls=%fused_computation.11.clone.1 | convolution fusion | flops 270598144 | bytes 4456464 | tf_op jit(solution)/shard_map/while/body/joh,jih->joi/dot_general | solution.py:30
  146.1 0.6 gather_fusion.1
  146.8 2.9 %gather_fusion.2 = bf16[4,128,2048]{2,1,0:T(8,128)(2,1)S(1)} fusion(bf16[8,128,2048]{2,1,0:T(8,128)(2,1)} %get-tuple-element.147, s32[1024]{0:T(1024)S(1)} %pad_clamp_fusion.8), kind=kCustom, calls=%fused_computation.3.clone.clone.1 | custom fusion | bytes 4194320 | tf_op jit(solution)/shard_map/while/body/jit(_take)/gather | solution.py:29
  149.7 4.2 %gather_fusion.3 = bf16[4,128,2048]{2,1,0:T(8,128)(2,1)} fusion(bf16[8,128,2048]{2,1,0:T(8,128)(2,1)} %get-tuple-element.147, s32[1024]{0:T(1024)S(1)} %pad_clamp_fusion.9), kind=kCustom, calls=%fused_computation.1.clone.clone.1 | custom fusion | bytes 4194320 | tf_op jit(solution)/shard_map/while/body/jit(_take)/gather | solution.py:28
  154.5 3.1 %fusion.28 = f32[24,128,128]{2,1,0:T(8,128)} fusion(f32[24,128,128]{2,1,0:T(8,128)} %get-tuple-element.132, s32[]{:T(128)S(6)} %select_n.118, bf16[4,128,2048]{2,1,0:T(8,128)(2,1)S(1)} %gather_fusion.2, pred[4]{0:T(512)(128)(4,1)S(1)} %get-tuple-element.117, bf16[4,128,2048]{2,1,0:T(8,128)(2,1)} %gather_fusion.3, ...), kind=kOutput, calls=%fused_computation.11.clone.1 | convolution fusion | flops 270598144 | bytes 4456464 | tf_op jit(solution)/shard_map/while/body/joh,jih->joi/dot_general | solution.py:30
  158.2 0.6 gather_fusion.1
  158.9 2.9 %gather_fusion.2 = bf16[4,128,2048]{2,1,0:T(8,128)(2,1)S(1)} fusion(bf16[8,128,2048]{2,1,0:T(8,128)(2,1)} %get-tuple-element.147, s32[1024]{0:T(1024)S(1)} %pad_clamp_fusion.8), kind=kCustom, calls=%fused_computation.3.clone.clone.1 | custom fusion | bytes 4194320 | tf_op jit(solution)/shard_map/while/body/jit(_take)/gather | solution.py:29
  161.8 4.2 %gather_fusion.3 = bf16[4,128,2048]{2,1,0:T(8,128)(2,1)} fusion(bf16[8,128,2048]{2,1,0:T(8,128)(2,1)} %get-tuple-element.147, s32[1024]{0:T(1024)S(1)} %pad_clamp_fusion.9), kind=kCustom, calls=%fused_computation.1.clone.clone.1 | custom fusion | bytes 4194320 | tf_op jit(solution)/shard_map/while/body/jit(_take)/gather | solution.py:28
  166.5 3.1 %fusion.28 = f32[24,128,128]{2,1,0:T(8,128)} fusion(f32[24,128,128]{2,1,0:T(8,128)} %get-tuple-element.132, s32[]{:T(128)S(6)} %select_n.118, bf16[4,128,2048]{2,1,0:T(8,128)(2,1)S(1)} %gather_fusion.2, pred[4]{0:T(512)(128)(4,1)S(1)} %get-tuple-element.117, bf16[4,128,2048]{2,1,0:T(8,128)(2,1)} %gather_fusion.3, ...), kind=kOutput, calls=%fused_computation.11.clone.1 | convolution fusion | flops 270598144 | bytes 4456464 | tf_op jit(solution)/shard_map/while/body/joh,jih->joi/dot_general | solution.py:30
  170.3 0.6 gather_fusion.1
  170.9 2.9 %gather_fusion.2 = bf16[4,128,2048]{2,1,0:T(8,128)(2,1)S(1)} fusion(bf16[8,128,2048]{2,1,0:T(8,128)(2,1)} %get-tuple-element.147, s32[1024]{0:T(1024)S(1)} %pad_clamp_fusion.8), kind=kCustom, calls=%fused_computation.3.clone.clone.1 | custom fusion | bytes 4194320 | tf_op jit(solution)/shard_map/while/body/jit(_take)/gather | solution.py:29
  173.8 4.2 %gather_fusion.3 = bf16[4,128,2048]{2,1,0:T(8,128)(2,1)} fusion(bf16[8,128,2048]{2,1,0:T(8,128)(2,1)} %get-tuple-element.147, s32[1024]{0:T(1024)S(1)} %pad_clamp_fusion.9), kind=kCustom, calls=%fused_computation.1.clone.clone.1 | custom fusion | bytes 4194320 | tf_op jit(solution)/shard_map/while/body/jit(_take)/gather | solution.py:28
  178.6 3.1 %fusion.28 = f32[24,128,128]{2,1,0:T(8,128)} fusion(f32[24,128,128]{2,1,0:T(8,128)} %get-tuple-element.132, s32[]{:T(128)S(6)} %select_n.118, bf16[4,128,2048]{2,1,0:T(8,128)(2,1)S(1)} %gather_fusion.2, pred[4]{0:T(512)(128)(4,1)S(1)} %get-tuple-element.117, bf16[4,128,2048]{2,1,0:T(8,128)(2,1)} %gather_fusion.3, ...), kind=kOutput, calls=%fused_computation.11.clone.1 | convolution fusion | flops 270598144 | bytes 4456464 | tf_op jit(solution)/shard_map/while/body/joh,jih->joi/dot_general | solution.py:30
  182.3 0.6 gather_fusion.1
  183.0 2.9 %gather_fusion.2 = bf16[4,128,2048]{2,1,0:T(8,128)(2,1)S(1)} fusion(bf16[8,128,2048]{2,1,0:T(8,128)(2,1)} %get-tuple-element.147, s32[1024]{0:T(1024)S(1)} %pad_clamp_fusion.8), kind=kCustom, calls=%fused_computation.3.clone.clone.1 | custom fusion | bytes 4194320 | tf_op jit(solution)/shard_map/while/body/jit(_take)/gather | solution.py:29
  185.9 4.2 %gather_fusion.3 = bf16[4,128,2048]{2,1,0:T(8,128)(2,1)} fusion(bf16[8,128,2048]{2,1,0:T(8,128)(2,1)} %get-tuple-element.147, s32[1024]{0:T(1024)S(1)} %pad_clamp_fusion.9), kind=kCustom, calls=%fused_computation.1.clone.clone.1 | custom fusion | bytes 4194320 | tf_op jit(solution)/shard_map/while/body/jit(_take)/gather | solution.py:28
  190.7 3.1 %fusion.28 = f32[24,128,128]{2,1,0:T(8,128)} fusion(f32[24,128,128]{2,1,0:T(8,128)} %get-tuple-element.132, s32[]{:T(128)S(6)} %select_n.118, bf16[4,128,2048]{2,1,0:T(8,128)(2,1)S(1)} %gather_fusion.2, pred[4]{0:T(512)(128)(4,1)S(1)} %get-tuple-element.117, bf16[4,128,2048]{2,1,0:T(8,128)(2,1)} %gather_fusion.3, ...), kind=kOutput, calls=%fused_computation.11.clone.1 | convolution fusion | flops 270598144 | bytes 4456464 | tf_op jit(solution)/shard_map/while/body/joh,jih->joi/dot_general | solution.py:30
  194.4 0.6 gather_fusion.1
  195.1 2.9 %gather_fusion.2 = bf16[4,128,2048]{2,1,0:T(8,128)(2,1)S(1)} fusion(bf16[8,128,2048]{2,1,0:T(8,128)(2,1)} %get-tuple-element.147, s32[1024]{0:T(1024)S(1)} %pad_clamp_fusion.8), kind=kCustom, calls=%fused_computation.3.clone.clone.1 | custom fusion | bytes 4194320 | tf_op jit(solution)/shard_map/while/body/jit(_take)/gather | solution.py:29
  198.0 4.2 %gather_fusion.3 = bf16[4,128,2048]{2,1,0:T(8,128)(2,1)} fusion(bf16[8,128,2048]{2,1,0:T(8,128)(2,1)} %get-tuple-element.147, s32[1024]{0:T(1024)S(1)} %pad_clamp_fusion.9), kind=kCustom, calls=%fused_computation.1.clone.clone.1 | custom fusion | bytes 4194320 | tf_op jit(solution)/shard_map/while/body/jit(_take)/gather | solution.py:28
  202.7 3.1 %fusion.28 = f32[24,128,128]{2,1,0:T(8,128)} fusion(f32[24,128,128]{2,1,0:T(8,128)} %get-tuple-element.132, s32[]{:T(128)S(6)} %select_n.118, bf16[4,128,2048]{2,1,0:T(8,128)(2,1)S(1)} %gather_fusion.2, pred[4]{0:T(512)(128)(4,1)S(1)} %get-tuple-element.117, bf16[4,128,2048]{2,1,0:T(8,128)(2,1)} %gather_fusion.3, ...), kind=kOutput, calls=%fused_computation.11.clone.1 | convolution fusion | flops 270598144 | bytes 4456464 | tf_op jit(solution)/shard_map/while/body/joh,jih->joi/dot_general | solution.py:30
  205.9 34.5 %reduce-scatter.2.cloned.1.call-done = f32[24,16,128]{2,1,0:T(8,128)} async-done(((f32[24,128,128]{2,1,0:T(8,128)}), f32[24,16,128]{2,1,0:T(8,128)}) %reduce-scatter.2.cloned.1.call-update) | async-done | bytes 196624 | tf_op jit(solution)/shard_map/reduce_scatter | solution.py:41
  (58 shorter events, 8.0 us)
Async XLA Ops:
  6.5 114.8 %all-gather.2.cloned.1.call-start = ((), (), s32[]{:S(2)}) async-start(), calls=%async_computation.1 | async-start | bytes 12582912 | tf_op jit(solution)/shard_map/all_gather | solution.py:17
  14.4 0.7 copy-start.3
  14.4 1.8 copy-start.2
  14.4 1.8 copy-start
  14.4 1.8 copy-start.1
  14.4 225.9 %reduce-scatter.2.cloned.1.call-start = ((), (), s32[]{:S(2)}) async-start(), calls=%async_computation.2 | async-start | bytes 1769472 | tf_op jit(solution)/shard_map/reduce_scatter | solution.py:41
Sparse Core Ops, SparseCore 0:
  14.5 106.6 all-gather.1
  206.0 34.3 reduce-scatter.1
where the time goes:
time: 248 us; the launch traced here: 247 us
  waiting for transfers between devices  140 us (56%)
  local copies, waits for them, and re-layouts  66.6 us (27%)
  matrix products  18.6 us (8%)
  between operations  14 us (6%)
  other arithmetic  8.21 us (3%)
    all_gather x1, waiting for transfers between devices, shards(): window_blocks = lax.all_gather(local_blocks, 'basis', axis=0, tiled=True)  105 us
    reduce_scatter x1, waiting for transfers between devices, shards(): lax.psum_scatter(partial_tiles, ('aux', 'occ'), scatter_dimension=1, tile...  34.5 us
    gather x12, local copies, waits for them, and re-layouts, single_round(): bra_block_rows = jnp.take(chosen, jnp.take(first_ids, clipped), axis=0)  29 us
    gather x12, local copies, waits for them, and re-layouts, single_round(): ket_block_rows = jnp.take(chosen, jnp.take(second_ids, clipped), axis=0)  21 us
    dot_general x6, matrix products, single_round(): jnp.einsum('joh,jih->joi', bra_block_rows, ket_block_rows, preferred_elem...  18.6 us
    reshape x1, local copies, waits for them, and re-layouts, shards(): local_blocks = integrals.reshape(blk_dev, BLK, width)  7.85 us
    gather x1, local copies, waits for them, and re-layouts, shards(): chosen = jnp.take(window_blocks, wanted, axis=0)  6.16 us
  transfers between devices with their start and end apart: 2, of which 2 were waited for; matrix products, arithmetic and copies ran while one was open for 0% of the time, Pallas kernels for 0%

commit v1 on v0

v1 whole, which is shorter than its diff:
```python
import functools

import jax
import jax.numpy as jnp
from jax import lax
from jax.experimental import pallas as pl
from jax.experimental.pallas import tpu as pltpu
from jax.sharding import PartitionSpec as P

BLK = 128
MESH = pl.DeviceIdType.MESH


def kernel(
    nb, nz, nc, per,
    need_ref, first_ref, second_ref, count_ref, x_ref,
    out_ref,
    xv, sent, held, mine, part, other, summed, come, total,
    load_sem, x_send, x_recv, c_send, c_recv, z_send, z_recv,
):
    b = lax.axis_index("basis")
    z = lax.axis_index("aux")
    c = lax.axis_index("occ")
    local = xv.shape[0]
    rows = part.shape[3]
    pmax = out_ref.shape[0]

    loads = []
    for i in range(local):
        load = pltpu.make_async_copy(x_ref.at[i], xv.at[i], load_sem.at[i])
        load.start()
        loads.append(load)

    x_peers = [lax.rem(b + s, nb) for s in range(1, nb)]
    z_peers = [lax.rem(z + o, nz) for o in range(1, nz)]
    c_peers = [lax.rem(c + o, nc) for o in range(1, nc)]
    barrier = pltpu.get_barrier_semaphore()
    for d in x_peers:
        pl.semaphore_signal(barrier, inc=1, device_id={"basis": d}, device_id_type=MESH)
    for d in z_peers:
        pl.semaphore_signal(barrier, inc=1, device_id={"aux": d}, device_id_type=MESH)
    for d in c_peers:
        pl.semaphore_signal(barrier, inc=1, device_id={"occ": d}, device_id_type=MESH)
    for load in loads:
        load.wait()
    pl.semaphore_wait(barrier, len(x_peers) + len(z_peers) + len(c_peers))

    def pack(owner, j, dst):
        block = lax.rem(need_ref[owner, b * per + j], local)

        def rows_of(r, _):
            at = pl.ds(pl.multiple_of(r * 32, 32), 32)
            dst[at, :] = xv[block, at, :]
            return 0

        lax.fori_loop(0, BLK // 32, rows_of, 0)

    pending = []
    for s in range(1, nb):
        d = lax.rem(b + nb - s, nb)
        for j in range(per):
            k = (s - 1) * per + j
            pack(d, j, sent.at[k])
            copy = pltpu.make_async_remote_copy(
                src_ref=sent.at[k],
                dst_ref=held.at[k],
                send_sem=x_send.at[k],
                recv_sem=x_recv.at[k],
                device_id={"basis": d},
                device_id_type=MESH,
            )
            copy.start()
            pending.append(copy)
    for j in range(per):
        pack(b, j, mine.at[j])

    def put(tile, slot):
        for q in range(nz * nc):
            part[q % nc, q // nc, slot] = tile[q * rows:(q + 1) * rows, :]

    def product(lhs, rhs):
        return lax.dot_general(
            lhs, rhs, (((1,), (1,)), ((), ())), preferred_element_type=jnp.float32
        )

    def exchange(step, lo, hi):
        copies = []
        for o, d in enumerate(c_peers):
            copy = pltpu.make_async_remote_copy(
                src_ref=part.at[d, :, lo:hi],
                dst_ref=other.at[o, :, lo:hi],
                send_sem=c_send.at[step, o],
                recv_sem=c_recv.at[step, o],
                device_id={"occ": d},
                device_id_type=MESH,
            )
            copy.start()
            copies.append(copy)
        return copies

    def spread(step, lo, hi):
        for slot in range(lo, hi):
            for q in range(nz):
                value = part[c, q, slot]
                for o in range(len(c_peers)):
                    value = value + other[o, q, slot]
                summed[q, slot] = value
        copies = []
        for o, d in enumerate(z_peers):
            copy = pltpu.make_async_remote_copy(
                src_ref=summed.at[d, lo:hi],
                dst_ref=come.at[o, lo:hi],
                send_sem=z_send.at[step, o],
                recv_sem=z_recv.at[step, o],
                device_id={"aux": d},
                device_id_type=MESH,
            )
            copy.start()
            copies.append(copy)
        return copies

    def finish(copies, lo, hi):
        for copy in copies:
            copy.wait()
        for slot in range(lo, hi):
            value = summed[z, slot]
            for o in range(len(z_peers)):
                value = value + come[o, slot]
            total[slot] = value

    def reduce(step, lo, hi):
        copies = exchange(step, lo, hi)
        for copy in copies:
            copy.wait()
        return spread(step, lo, hi)

    for a in range(1, per):
        for e in range(a):
            put(product(mine[e], mine[a]), a * (a - 1) // 2 + e)
    waiting = None
    lo, hi = 0, per * (per - 1) // 2
    waiting = (reduce(0, lo, hi), lo, hi)
    for a in range(per, nb * per):
        k = a - per
        s = a // per
        wrap = (b + s) // nb
        pending[k].wait_recv()
        base = a * (a - 1) // 2

        @pl.when(wrap == 0)
        def _():
            for e in range(per):
                put(product(mine[e], held[k]), base + e)

        @pl.when(wrap != 0)
        def _():
            for e in range(per):
                put(product(held[k], mine[e]), base + e)

        for e in range(per, a):
            flip = wrap - (b + e // per) // nb
            first = (e - per) + flip * (a - e)
            second = k - flip * (a - e)
            put(product(held[first], held[second]), base + e)
        lo, hi = base, base + a
        moving = reduce(a - per + 1, lo, hi)
        finish(*waiting)
        waiting = (moving, lo, hi)
    finish(*waiting)
    for copy in pending:
        copy.wait_send()

    live = count_ref[b]
    for p in range(pmax):
        u = first_ref[b, p]
        v = second_ref[b, p]
        u = lax.rem(u // per - b + nb, nb) * per + lax.rem(u, per)
        v = lax.rem(v // per - b + nb, nb) * per + lax.rem(v, per)
        big = jnp.maximum(u, v)
        small = jnp.minimum(u, v)
        value = total[jnp.minimum(big * (big - 1) // 2 + small, total.shape[0] - 1)]
        out_ref[p] = jnp.where(p < live, value, jnp.zeros_like(value))


def shards(mesh, integrals, need_blocks, pair_first, pair_second, pair_count):
    nb, nz, nc = mesh.shape["basis"], mesh.shape["aux"], mesh.shape["occ"]
    size, aux_size, occ_size = integrals.shape
    local = size // BLK
    width = aux_size * occ_size
    pmax = pair_first.shape[1]
    blocks = need_blocks.shape[1]
    per = blocks // nb
    slots = blocks * (blocks - 1) // 2
    rows = BLK // (nz * nc)
    steps = 1 + blocks - per
    x = integrals.reshape(local, BLK, width)
    f32, bf16 = jnp.float32, jnp.bfloat16
    out = pl.pallas_call(
        functools.partial(kernel, nb, nz, nc, per),
        out_shape=jax.ShapeDtypeStruct((pmax, rows, BLK), f32),
        in_specs=[pl.BlockSpec(memory_space=pltpu.SMEM)] * 4 + [pl.BlockSpec(memory_space=pl.ANY)],
        out_specs=pl.BlockSpec(memory_space=pltpu.VMEM),
        scratch_shapes=[
            pltpu.VMEM((local, BLK, width), bf16),
            pltpu.VMEM((blocks - per, BLK, width), bf16),
            pltpu.VMEM((blocks - per, BLK, width), bf16),
            pltpu.VMEM((per, BLK, width), bf16),
            pltpu.VMEM((nc, nz, slots, rows, BLK), f32),
            pltpu.VMEM((nc - 1, nz, slots, rows, BLK), f32),
            pltpu.VMEM((nz, slots, rows, BLK), f32),
            pltpu.VMEM((nz - 1, slots, rows, BLK), f32),
            pltpu.VMEM((slots, rows, BLK), f32),
            pltpu.SemaphoreType.DMA((local,)),
            pltpu.SemaphoreType.DMA((blocks - per,)),
            pltpu.SemaphoreType.DMA((blocks - per,)),
            pltpu.SemaphoreType.DMA((steps, nc - 1)),
            pltpu.SemaphoreType.DMA((steps, nc - 1)),
            pltpu.SemaphoreType.DMA((steps, nz - 1)),
            pltpu.SemaphoreType.DMA((steps, nz - 1)),
        ],
        compiler_params=pltpu.CompilerParams(
            collective_id=0, has_side_effects=True, vmem_limit_bytes=48 * 2**20
        ),
    )(need_blocks, pair_first, pair_second, pair_count, x)
    return out[None]


def solution(mesh):
    in_specs = (
        P(("groups", "basis"), "aux", "occ"),
        P("groups", None),
        P("groups", None),
        P("groups", None),
        P("groups"),
    )
    out_specs = P(("groups", "basis"), None, ("aux", "occ"), None)
    return jax.shard_map(
        functools.partial(shards, mesh), mesh=mesh, in_specs=in_specs, out_specs=out_specs, check_vma=False
    )
```

time: 248 us -> 73.3 us (0.30)
  waiting for transfers between devices: 140 us -> 0 us
  Pallas kernels: 0 us -> 62.2 us
  local copies, waits for them, and re-layouts: 66.6 us -> 10.7 us
  matrix products: 18.6 us -> 0 us
  between operations: 14 us -> 0.03 us
  other arithmetic: 8.21 us -> 0 us
    all_gather x1 -> x0, waiting for transfers between devices: 105 us -> none  [shards(): window_blocks = lax.all_gather(local_blocks, 'basis', axis=0, tiled=True)]
    pallas_call x0 -> x1, Pallas kernels: none -> 62.2 us  [shards(): pl.pallas_call(functools.partial(kernel, nb, nz, nc, per), out_shape=jax....]
    gather x25 -> x0, local copies, waits for them, and re-layouts: 56.3 us -> none  [the longest x12 29 us: single_round(): bra_block_rows = jnp.take(chosen, jnp.take(first_ids, clipped), axis=0)]
    reduce_scatter x1 -> x0, waiting for transfers between devices: 34.5 us -> none  [shards(): lax.psum_scatter(partial_tiles, ('aux', 'occ'), scatter_dimension=1, tile...]
    dot_general x6 -> x0, matrix products: 18.6 us -> none  [single_round(): jnp.einsum('joh,jih->joi', bra_block_rows, ket_block_rows, preferred_elem...]
    select_n x8 -> x0, other arithmetic: 4.66 us -> none  [the longest x2 4.63 us: shards(): chosen = jnp.take(window_blocks, wanted, axis=0)]
    lt x6 -> x0, other arithmetic: 3.32 us -> none  [single_round(): slot_indices < surviving_count]
  transfers between devices with their start and end apart: 2 -> 0, of which waited for: 2 -> 0; matrix products, arithmetic and copies ran while one was open for 0% -> 0% of each run, Pallas kernels for 0% -> 0%
where the time goes in v1:
time: 73.3 us; the launch traced here: 73 us
  Pallas kernels  62.2 us (85%)
  local copies, waits for them, and re-layouts  10.7 us (15%)
    pallas_call x1, Pallas kernels, shards(): pl.pallas_call(functools.partial(kernel, nb, nz, nc, per), out_shape=jax....  62.2 us
    reshape x1, local copies, waits for them, and re-layouts, shards(): x = integrals.reshape(local, BLK, width)  7.83 us
    unnamed x11, local copies, waits for them, and re-layouts  2.88 us

profile of v1, /device:TPU:0, one launch (start us, length us, event | category | flops | bytes accessed | tf_op | source)
XLA Modules:
  0.0 73.0 jit_solution(17982584086678490997)
XLA Ops:
  0.0 0.0 copy-start.4
  0.0 0.0 copy-start.3
  0.0 0.0 copy-start.2
  0.0 0.0 copy-start.1
  0.0 7.8 %reshape.3.x_ref = bf16[8,128,2048]{2,1,0:T(8,128)(2,1)} reshape(bf16[1024,2,1024]{2,1,0:T(2,128)(2,1)} %param.5) | data formatting | bytes 8388608 | tf_op jit(solution)/shard_map/reshape | solution.py:196
  7.8 0.0 copy-done.4
  7.8 0.0 copy-done.3
  7.8 0.0 copy-done.2
  7.9 0.0 copy-done.1
  7.9 0.0 copy-start
  7.9 2.2 %copy-done = bf16[8,128,2048]{2,1,0:T(8,128)(2,1)S(1)} copy-done((bf16[8,128,2048]{2,1,0:T(8,128)(2,1)S(1)}, bf16[8,128,2048]{2,1,0:T(8,128)(2,1)}, u32[]{:S(2)}) %copy-start) | copy-done | bytes 4194328
  10.1 62.2 %shard_map.55 = f32[24,16,128]{2,1,0:T(8,128)S(1)} custom-call(s32[2,8]{1,0:T(2,128)S(1)} %copy-done.1, s32[2,24]{1,0:T(2,128)S(1)} %copy-done.2, s32[2,24]{1,0:T(2,128)S(1)} %copy-done.3, s32[2]{0:T(128)S(1)} %copy-done.4, bf16[8,128,2048]{2,1,0:T(8,128)(2,1)S(1)} %copy-done), custom_call_target="tpu_custom_call" | custom-call | tf_op jit(solution)/shard_map/pallas_call | solution.py:198
  72.3 0.7 copy.7
Async XLA Ops:
  0.0 7.8 %copy-start.4 = (s32[2]{0:T(128)S(1)}, s32[2]{0:T(128)}, u32[]{:S(2)}) copy-start(s32[2]{0:T(128)} %count_ref.1) | copy-start | bytes 28
  0.0 7.8 %copy-start.3 = (s32[2,24]{1,0:T(2,128)S(1)}, s32[2,24]{1,0:T(2,128)}, u32[]{:S(2)}) copy-start(s32[2,24]{1,0:T(2,128)} %second_ref.1) | copy-start | bytes 580
  0.0 7.8 %copy-start.2 = (s32[2,24]{1,0:T(2,128)S(1)}, s32[2,24]{1,0:T(2,128)}, u32[]{:S(2)}) copy-start(s32[2,24]{1,0:T(2,128)} %first_ref.1) | copy-start | bytes 580
  0.0 7.8 %copy-start.1 = (s32[2,8]{1,0:T(2,128)S(1)}, s32[2,8]{1,0:T(2,128)}, u32[]{:S(2)}) copy-start(s32[2,8]{1,0:T(2,128)} %need_ref.1) | copy-start | bytes 196
  7.9 2.2 %copy-start = (bf16[8,128,2048]{2,1,0:T(8,128)(2,1)S(1)}, bf16[8,128,2048]{2,1,0:T(8,128)(2,1)}, u32[]{:S(2)}) copy-start(bf16[8,128,2048]{2,1,0:T(8,128)(2,1)} %reshape.3.x_ref) | copy-start | bytes 12582916

commit v2 on v1

--- a/solution.py
+++ b/solution.py
@@ -8,6 +8,7 @@
 from jax.sharding import PartitionSpec as P
 
 BLK = 128
+CUT = 4
 MESH = pl.DeviceIdType.MESH
 
 
@@ -50,29 +51,33 @@
 
         def rows_of(r, _):
             at = pl.ds(pl.multiple_of(r * 32, 32), 32)
-            dst[at, :] = xv[block, at, :]
+            dst[at, :] = xv[block, at].reshape(32, dst.shape[1])
             return 0
 
         lax.fori_loop(0, BLK // 32, rows_of, 0)
 
     pending = []
+    piece = BLK // CUT
     for s in range(1, nb):
         d = lax.rem(b + nb - s, nb)
         for j in range(per):
             k = (s - 1) * per + j
             pack(d, j, sent.at[k])
-            copy = pltpu.make_async_remote_copy(
-                src_ref=sent.at[k],
-                dst_ref=held.at[k],
-                send_sem=x_send.at[k],
-                recv_sem=x_recv.at[k],
-                device_id={"basis": d},
-                device_id_type=MESH,
-            )
-            copy.start()
-            pending.append(copy)
+            for i in range(CUT):
+                at = pl.ds(i * piece, piece)
+                copy = pltpu.make_async_remote_copy(
+                    src_ref=sent.at[k, at],
+                    dst_ref=held.at[k, at],
+                    send_sem=x_send.at[k, i],
+                    recv_sem=x_recv.at[k, i],
+                    device_id={"basis": d},
+                    device_id_type=MESH,
+                )
+                pending.append(copy)
+                if len(pending) <= CUT:
+                    copy.start()
     for j in range(per):
-        pack(b, j, mine.at[j])
+        pack(b, j, mine.at[pl.ds(j * BLK, BLK)])
 
     def put(tile, slot):
         for q in range(nz * nc):
@@ -134,9 +139,12 @@
             copy.wait()
         return spread(step, lo, hi)
 
+    def own(j):
+        return mine[j * BLK:(j + 1) * BLK, :]
+
     for a in range(1, per):
         for e in range(a):
-            put(product(mine[e], mine[a]), a * (a - 1) // 2 + e)
+            put(product(own(e), own(a)), a * (a - 1) // 2 + e)
     waiting = None
     lo, hi = 0, per * (per - 1) // 2
     waiting = (reduce(0, lo, hi), lo, hi)
@@ -144,18 +152,23 @@
         k = a - per
         s = a // per
         wrap = (b + s) // nb
-        pending[k].wait_recv()
+        for i in range(k * CUT, (k + 1) * CUT):
+            pending[i].wait_recv()
+            if i + CUT < len(pending):
+                pending[i + CUT].start()
         base = a * (a - 1) // 2
 
         @pl.when(wrap == 0)
         def _():
+            wide = product(mine[...], held[k])
             for e in range(per):
-                put(product(mine[e], held[k]), base + e)
+                put(wide[e * BLK:(e + 1) * BLK, :], base + e)
 
         @pl.when(wrap != 0)
         def _():
+            wide = product(held[k], mine[...])
             for e in range(per):
-                put(product(held[k], mine[e]), base + e)
+                put(wide[:, e * BLK:(e + 1) * BLK], base + e)
 
         for e in range(per, a):
             flip = wrap - (b + e // per) // nb
@@ -193,33 +206,33 @@
     slots = blocks * (blocks - 1) // 2
     rows = BLK // (nz * nc)
     steps = 1 + blocks - per
-    x = integrals.reshape(local, BLK, width)
+    x = integrals.reshape(local, BLK, aux_size, occ_size)
     f32, bf16 = jnp.float32, jnp.bfloat16
     out = pl.pallas_call(
         functools.partial(kernel, nb, nz, nc, per),
         out_shape=jax.ShapeDtypeStruct((pmax, rows, BLK), f32),
-        in_specs=[pl.BlockSpec(memory_space=pltpu.SMEM)] * 4 + [pl.BlockSpec(memory_space=pl.ANY)],
+        in_specs=[pl.BlockSpec(memory_space=pltpu.SMEM)] * 4 + [pl.BlockSpec(memory_space=pltpu.HBM)],
         out_specs=pl.BlockSpec(memory_space=pltpu.VMEM),
         scratch_shapes=[
-            pltpu.VMEM((local, BLK, width), bf16),
+            pltpu.VMEM((local, BLK, aux_size, occ_size), bf16),
             pltpu.VMEM((blocks - per, BLK, width), bf16),
             pltpu.VMEM((blocks - per, BLK, width), bf16),
-            pltpu.VMEM((per, BLK, width), bf16),
+            pltpu.VMEM((per * BLK, width), bf16),
             pltpu.VMEM((nc, nz, slots, rows, BLK), f32),
             pltpu.VMEM((nc - 1, nz, slots, rows, BLK), f32),
             pltpu.VMEM((nz, slots, rows, BLK), f32),
             pltpu.VMEM((nz - 1, slots, rows, BLK), f32),
             pltpu.VMEM((slots, rows, BLK), f32),
             pltpu.SemaphoreType.DMA((local,)),
-            pltpu.SemaphoreType.DMA((blocks - per,)),
-            pltpu.SemaphoreType.DMA((blocks - per,)),
+            pltpu.SemaphoreType.DMA((blocks - per, CUT)),
+            pltpu.SemaphoreType.DMA((blocks - per, CUT)),
             pltpu.SemaphoreType.DMA((steps, nc - 1)),
             pltpu.SemaphoreType.DMA((steps, nc - 1)),
             pltpu.SemaphoreType.DMA((steps, nz - 1)),
             pltpu.SemaphoreType.DMA((steps, nz - 1)),
         ],
         compiler_params=pltpu.CompilerParams(
-            collective_id=0, has_side_effects=True, vmem_limit_bytes=48 * 2**20
+            collective_id=0, has_side_effects=True, vmem_limit_bytes=61 * 2**20
         ),
     )(need_blocks, pair_first, pair_second, pair_count, x)
     return out[None]

time: 73.3 us -> 65.6 us (0.89)
  local copies, waits for them, and re-layouts: 10.7 us -> 1.62 us
  Pallas kernels: 62.2 us -> 63.8 us
    reshape x1 -> x0, local copies, waits for them, and re-layouts: 7.83 us -> none  [shards(): x = integrals.reshape(local, BLK, width)]
    pallas_call x1, Pallas kernels: 62.2 us -> 63.8 us  [shards(): pl.pallas_call(functools.partial(kernel, nb, nz, nc, per), out_shape=jax....]
    unnamed x11 -> x1, local copies, waits for them, and re-layouts: 2.88 us -> 1.62 us
where the time goes in v2:
time: 65.6 us; the launch traced here: 65.4 us
  Pallas kernels  63.8 us (97%)
  local copies, waits for them, and re-layouts  1.62 us (2%)
    pallas_call x1, Pallas kernels, shards(): pl.pallas_call(functools.partial(kernel, nb, nz, nc, per), out_shape=jax....  63.8 us
    unnamed x1, local copies, waits for them, and re-layouts  1.62 us

profile of v2, /device:TPU:0, one launch (start us, length us, event | category | flops | bytes accessed | tf_op | source)
XLA Modules:
  0.0 65.4 jit_solution(6308677356991454024)
XLA Ops:
  0.0 63.8 %shard_map.55 = f32[24,16,128]{2,1,0:T(8,128)} custom-call(s32[2,8]{1,0:T(2,128)} %need_ref.1, s32[2,24]{1,0:T(2,128)} %first_ref.1, s32[2,24]{1,0:T(2,128)} %second_ref.1, s32[2]{0:T(128)} %count_ref.1, bf16[8,128,2,1024]{3,2,1,0:T(2,128)(2,1)} %bitcast.2), custom_call_target="tpu_custom_call" | custom-call | tf_op jit(solution)/shard_map/pallas_call | solution.py:211
  63.8 1.6 %copy.7 = f32[1,24,16,128]{3,2,1,0:T(8,128)} copy(f32[1,24,16,128]{3,2,1,0:T(8,128)} %bitcast.3) | data formatting | bytes 393216

commit v3 on v2

--- a/solution.py
+++ b/solution.py
@@ -14,21 +14,31 @@
 
 def kernel(
     nb, nz, nc, per,
-    need_ref, first_ref, second_ref, count_ref, x_ref,
+    need_in, first_in, second_in, count_in, x_ref,
     out_ref,
-    xv, sent, held, mine, part, other, summed, come, total,
-    load_sem, x_send, x_recv, c_send, c_recv, z_send, z_recv,
+    need_ref, first_ref, second_ref, count_ref, *rest,
 ):
+    xv, rest = rest[:CUT], rest[CUT:]
+    sent, held, mine, part, other, summed, come, total = rest[:8]
+    load_sem, arg_sem, x_send, x_recv, c_send, c_recv, z_send, z_recv = rest[8:]
     b = lax.axis_index("basis")
     z = lax.axis_index("aux")
     c = lax.axis_index("occ")
-    local = xv.shape[0]
+    local = x_ref.shape[0]
+    piece = BLK // CUT
     rows = part.shape[3]
     pmax = out_ref.shape[0]
 
+    tables = []
+    for i, (src, dst) in enumerate((
+        (need_in, need_ref), (first_in, first_ref), (second_in, second_ref), (count_in, count_ref)
+    )):
+        table = pltpu.make_async_copy(src, dst, arg_sem.at[i])
+        table.start()
+        tables.append(table)
     loads = []
-    for i in range(local):
-        load = pltpu.make_async_copy(x_ref.at[i], xv.at[i], load_sem.at[i])
+    for i in range(CUT):
+        load = pltpu.make_async_copy(x_ref.at[:, pl.ds(i * piece, piece)], xv[i], load_sem.at[i])
         load.start()
         loads.append(load)
 
@@ -42,29 +52,23 @@
         pl.semaphore_signal(barrier, inc=1, device_id={"aux": d}, device_id_type=MESH)
     for d in c_peers:
         pl.semaphore_signal(barrier, inc=1, device_id={"occ": d}, device_id_type=MESH)
-    for load in loads:
-        load.wait()
+    tables[0].wait()
     pl.semaphore_wait(barrier, len(x_peers) + len(z_peers) + len(c_peers))
 
-    def pack(owner, j, dst):
+    def pack(owner, j, i, dst):
         block = lax.rem(need_ref[owner, b * per + j], local)
-
-        def rows_of(r, _):
-            at = pl.ds(pl.multiple_of(r * 32, 32), 32)
-            dst[at, :] = xv[block, at].reshape(32, dst.shape[1])
-            return 0
-
-        lax.fori_loop(0, BLK // 32, rows_of, 0)
+        dst[...] = xv[i][block].reshape(piece, dst.shape[1])
 
     pending = []
-    piece = BLK // CUT
     for s in range(1, nb):
         d = lax.rem(b + nb - s, nb)
         for j in range(per):
             k = (s - 1) * per + j
-            pack(d, j, sent.at[k])
             for i in range(CUT):
                 at = pl.ds(i * piece, piece)
+                if len(pending) < CUT:
+                    loads[i].wait()
+                pack(d, j, i, sent.at[k, at])
                 copy = pltpu.make_async_remote_copy(
                     src_ref=sent.at[k, at],
                     dst_ref=held.at[k, at],
@@ -77,7 +81,8 @@
                 if len(pending) <= CUT:
                     copy.start()
     for j in range(per):
-        pack(b, j, mine.at[pl.ds(j * BLK, BLK)])
+        for i in range(CUT):
+            pack(b, j, i, mine.at[pl.ds(j * BLK + i * piece, piece)])
 
     def put(tile, slot):
         for q in range(nz * nc):
@@ -183,6 +188,8 @@
     for copy in pending:
         copy.wait_send()
 
+    for table in tables[1:]:
+        table.wait()
     live = count_ref[b]
     for p in range(pmax):
         u = first_ref[b, p]
@@ -211,10 +218,14 @@
     out = pl.pallas_call(
         functools.partial(kernel, nb, nz, nc, per),
         out_shape=jax.ShapeDtypeStruct((pmax, rows, BLK), f32),
-        in_specs=[pl.BlockSpec(memory_space=pltpu.SMEM)] * 4 + [pl.BlockSpec(memory_space=pltpu.HBM)],
+        in_specs=[pl.BlockSpec(memory_space=pltpu.HBM)] * 5,
         out_specs=pl.BlockSpec(memory_space=pltpu.VMEM),
         scratch_shapes=[
-            pltpu.VMEM((local, BLK, aux_size, occ_size), bf16),
+            *[
+                pltpu.SMEM(table.shape, jnp.int32)
+                for table in (need_blocks, pair_first, pair_second, pair_count)
+            ],
+            *[pltpu.VMEM((local, BLK // CUT, aux_size, occ_size), bf16)] * CUT,
             pltpu.VMEM((blocks - per, BLK, width), bf16),
             pltpu.VMEM((blocks - per, BLK, width), bf16),
             pltpu.VMEM((per * BLK, width), bf16),
@@ -223,7 +234,8 @@
             pltpu.VMEM((nz, slots, rows, BLK), f32),
             pltpu.VMEM((nz - 1, slots, rows, BLK), f32),
             pltpu.VMEM((slots, rows, BLK), f32),
-            pltpu.SemaphoreType.DMA((local,)),
+            pltpu.SemaphoreType.DMA((CUT,)),
+            pltpu.SemaphoreType.DMA((4,)),
             pltpu.SemaphoreType.DMA((blocks - per, CUT)),
             pltpu.SemaphoreType.DMA((blocks - per, CUT)),
             pltpu.SemaphoreType.DMA((steps, nc - 1)),

time: 65.6 us -> 64 us (0.976)
  Pallas kernels: 63.8 us -> 62.2 us
    pallas_call x1, Pallas kernels: 63.8 us -> 62.2 us  [shards(): pl.pallas_call(functools.partial(kernel, nb, nz, nc, per), out_shape=jax....]
where the time goes in v3:
time: 64 us; the launch traced here: 63.8 us
  Pallas kernels  62.2 us (97%)
  local copies, waits for them, and re-layouts  1.62 us (3%)
    pallas_call x1, Pallas kernels, shards(): pl.pallas_call(functools.partial(kernel, nb, nz, nc, per), out_shape=jax....  62.2 us
    unnamed x1, local copies, waits for them, and re-layouts  1.62 us

profile of v3, /device:TPU:0, one launch (start us, length us, event | category | flops | bytes accessed | tf_op | source)
XLA Modules:
  0.0 63.8 jit_solution(4563133268764062756)
XLA Ops:
  0.0 62.2 %shard_map.55 = f32[24,16,128]{2,1,0:T(8,128)} custom-call(s32[2,8]{1,0:T(2,128)} %need_in.1, s32[2,24]{1,0:T(2,128)} %first_in.1, s32[2,24]{1,0:T(2,128)} %second_in.1, s32[2]{0:T(128)} %count_in.1, bf16[8,128,2,1024]{3,2,1,0:T(2,128)(2,1)} %bitcast.2), custom_call_target="tpu_custom_call" | custom-call | tf_op jit(solution)/shard_map/pallas_call | solution.py:218
  62.2 1.6 %copy.7 = f32[1,24,16,128]{3,2,1,0:T(8,128)} copy(f32[1,24,16,128]{3,2,1,0:T(8,128)} %bitcast.3) | data formatting | bytes 393216

commit v4 on v3

--- a/solution.py
+++ b/solution.py
@@ -13,14 +13,14 @@
 
 
 def kernel(
-    nb, nz, nc, per,
+    nb, nz, nc, per, split,
     need_in, first_in, second_in, count_in, x_ref,
     out_ref,
     need_ref, first_ref, second_ref, count_ref, *rest,
 ):
     xv, rest = rest[:CUT], rest[CUT:]
-    sent, held, mine, part, other, summed, come, total = rest[:8]
-    load_sem, arg_sem, x_send, x_recv, c_send, c_recv, z_send, z_recv = rest[8:]
+    sent, held, mine, part, other, summed, come, total, spare = rest[:9]
+    load_sem, arg_sem, x_send, x_recv, c_send, c_recv, z_send, z_recv, g_send, g_recv = rest[9:]
     b = lax.axis_index("basis")
     z = lax.axis_index("aux")
     c = lax.axis_index("occ")
@@ -59,6 +59,15 @@
         block = lax.rem(need_ref[owner, b * per + j], local)
         dst[...] = xv[i][block].reshape(piece, dst.shape[1])
 
+    def pack_strided(owner, j, i, dst):
+        block = lax.rem(need_ref[owner, b * per + j], local)
+        h, quarter = i // 2, i % 2
+        taken = []
+        for n in range(4):
+            row = 16 * (4 * quarter + n) + 8 * h
+            taken.append(xv[row // piece][block, row % piece:row % piece + 8])
+        dst[...] = jnp.concatenate(taken, axis=0).reshape(piece, dst.shape[1])
+
     pending = []
     for s in range(1, nb):
         d = lax.rem(b + nb - s, nb)
@@ -68,7 +77,18 @@
                 at = pl.ds(i * piece, piece)
                 if len(pending) < CUT:
                     loads[i].wait()
-                pack(d, j, i, sent.at[k, at])
+                if split and k == per - 1:
+                    @pl.when(d == 0)
+                    def _():
+                        pack(d, j, i, sent.at[k, at])
+
+                    @pl.when(d != 0)
+                    def _():
+                        pack_strided(d, j, i, sent.at[k, at])
+
+                    pack(d, j, i, spare.at[at])
+                else:
+                    pack(d, j, i, sent.at[k, at])
                 copy = pltpu.make_async_remote_copy(
                     src_ref=sent.at[k, at],
                     dst_ref=held.at[k, at],
@@ -150,18 +170,35 @@
     for a in range(1, per):
         for e in range(a):
             put(product(own(e), own(a)), a * (a - 1) // 2 + e)
-    waiting = None
     lo, hi = 0, per * (per - 1) // 2
-    waiting = (reduce(0, lo, hi), lo, hi)
+    waiting = [(reduce(0, lo, hi), lo, hi)]
+    step = 1
+    give = None
+    if split:
+        base = total.shape[0] - (per - 1)
+        for e in range(per - 1):
+            put(product(sent[e], spare[...]), base + e)
+        waiting.append((reduce(step, base, base + per - 1), base, base + per - 1))
+        step += 1
+        give = pltpu.make_async_remote_copy(
+            src_ref=total.at[base:base + per - 1],
+            dst_ref=total.at[base - (per - 1):base],
+            send_sem=g_send,
+            recv_sem=g_recv,
+            device_id={"basis": x_peers[0]},
+            device_id_type=MESH,
+        )
     for a in range(per, nb * per):
         k = a - per
         s = a // per
         wrap = (b + s) // nb
+        base = a * (a - 1) // 2
+        if split and a == nb * per - 1:
+            break
         for i in range(k * CUT, (k + 1) * CUT):
             pending[i].wait_recv()
             if i + CUT < len(pending):
                 pending[i + CUT].start()
-        base = a * (a - 1) // 2
 
         @pl.when(wrap == 0)
         def _():
@@ -181,15 +218,74 @@
             second = k - flip * (a - e)
             put(product(held[first], held[second]), base + e)
         lo, hi = base, base + a
-        moving = reduce(a - per + 1, lo, hi)
-        finish(*waiting)
-        waiting = (moving, lo, hi)
-    finish(*waiting)
+        moving = reduce(step, lo, hi)
+        step += 1
+        for move in waiting:
+            finish(*move)
+        waiting = [(moving, lo, hi)]
+        if split and a == per:
+            give.start()
+    if split:
+        half = BLK // 2
+        for h in range(2):
+            for i in range(k * CUT + 2 * h, k * CUT + 2 * h + 2):
+                pending[i].wait_recv()
+            at = slice(h * half, (h + 1) * half)
+
+            @pl.when(wrap == 0)
+            def _():
+                wide = product(mine[...], held[k, at])
+                for m in range(per // 2):
+                    left = wide[2 * m * BLK:(2 * m + 1) * BLK, :]
+                    right = wide[(2 * m + 1) * BLK:(2 * m + 2) * BLK, :]
+                    put(jnp.concatenate([left, right], axis=1), base + h * per // 2 + m)
+
+            @pl.when(wrap != 0)
+            def _():
+                wide = product(held[k, at], mine[...])
+                for m in range(per // 2):
+                    for q in range(nz * nc):
+                        for n in range(2):
+                            e = 2 * m + n
+                            part[q % nc, q // nc, base + h * per // 2 + m, 8 * n:8 * n + 8] = (
+                                wide[8 * q:8 * q + 8, e * BLK:(e + 1) * BLK]
+                            )
+
+            lo, hi = base + h * per // 2, base + (h + 1) * per // 2
+            moving = reduce(step, lo, hi)
+            step += 1
+            for move in waiting:
+                finish(*move)
+            waiting = [(moving, lo, hi)]
+    for move in waiting:
+        finish(*move)
+    if split:
+        shares = [total[base + i] for i in range(per)]
+
+        @pl.when(wrap == 0)
+        def _():
+            for e in range(per):
+                n, m = e % 2, e // 2
+                total[base + e] = jnp.concatenate(
+                    [shares[m][:, n * half:(n + 1) * half], shares[per // 2 + m][:, n * half:(n + 1) * half]],
+                    axis=1,
+                )
+
+        @pl.when(wrap != 0)
+        def _():
+            for e in range(per):
+                n, m = e % 2, e // 2
+                total[base + e] = jnp.concatenate(
+                    [shares[m][8 * n:8 * n + 8], shares[per // 2 + m][8 * n:8 * n + 8]], axis=0
+                )
+
+        give.wait()
     for copy in pending:
         copy.wait_send()
 
     for table in tables[1:]:
         table.wait()
+    first_slots = nb * per * (nb * per - 1) // 2
     live = count_ref[b]
     for p in range(pmax):
         u = first_ref[b, p]
@@ -198,7 +294,7 @@
         v = lax.rem(v // per - b + nb, nb) * per + lax.rem(v, per)
         big = jnp.maximum(u, v)
         small = jnp.minimum(u, v)
-        value = total[jnp.minimum(big * (big - 1) // 2 + small, total.shape[0] - 1)]
+        value = total[jnp.minimum(big * (big - 1) // 2 + small, first_slots - 1)]
         out_ref[p] = jnp.where(p < live, value, jnp.zeros_like(value))
 
 
@@ -212,11 +308,13 @@
     per = blocks // nb
     slots = blocks * (blocks - 1) // 2
     rows = BLK // (nz * nc)
-    steps = 1 + blocks - per
+    split = nb == 2 and per == 4 and rows == 16
+    slots += per - 1 if split else 0
+    steps = 3 + blocks - per
     x = integrals.reshape(local, BLK, aux_size, occ_size)
     f32, bf16 = jnp.float32, jnp.bfloat16
     out = pl.pallas_call(
-        functools.partial(kernel, nb, nz, nc, per),
+        functools.partial(kernel, nb, nz, nc, per, split),
         out_shape=jax.ShapeDtypeStruct((pmax, rows, BLK), f32),
         in_specs=[pl.BlockSpec(memory_space=pltpu.HBM)] * 5,
         out_specs=pl.BlockSpec(memory_space=pltpu.VMEM),
@@ -234,6 +332,7 @@
             pltpu.VMEM((nz, slots, rows, BLK), f32),
             pltpu.VMEM((nz - 1, slots, rows, BLK), f32),
             pltpu.VMEM((slots, rows, BLK), f32),
+            pltpu.VMEM((BLK, width), bf16),
             pltpu.SemaphoreType.DMA((CUT,)),
             pltpu.SemaphoreType.DMA((4,)),
             pltpu.SemaphoreType.DMA((blocks - per, CUT)),
@@ -242,6 +341,8 @@
             pltpu.SemaphoreType.DMA((steps, nc - 1)),
             pltpu.SemaphoreType.DMA((steps, nz - 1)),
             pltpu.SemaphoreType.DMA((steps, nz - 1)),
+            pltpu.SemaphoreType.DMA,
+            pltpu.SemaphoreType.DMA,
         ],
         compiler_params=pltpu.CompilerParams(
             collective_id=0, has_side_effects=True, vmem_limit_bytes=61 * 2**20

time: 64 us -> 61.5 us (0.961)
  Pallas kernels: 62.2 us -> 59.8 us
    pallas_call x1, Pallas kernels: 62.2 us -> 59.8 us  [shards(): pl.pallas_call(functools.partial(kernel, nb, nz, nc, per, split), out_sha...]
where the time goes in v4:
time: 61.5 us; the launch traced here: 61.4 us
  Pallas kernels  59.8 us (97%)
  local copies, waits for them, and re-layouts  1.62 us (3%)
    pallas_call x1, Pallas kernels, shards(): pl.pallas_call(functools.partial(kernel, nb, nz, nc, per, split), out_sha...  59.8 us
    unnamed x1, local copies, waits for them, and re-layouts  1.62 us

profile of v4, /device:TPU:0, one launch (start us, length us, event | category | flops | bytes accessed | tf_op | source)
XLA Modules:
  0.0 61.4 jit_solution(8414496089353334626)
XLA Ops:
  0.0 59.8 %shard_map.55 = f32[24,16,128]{2,1,0:T(8,128)} custom-call(s32[2,8]{1,0:T(2,128)} %need_in.1, s32[2,24]{1,0:T(2,128)} %first_in.1, s32[2,24]{1,0:T(2,128)} %second_in.1, s32[2]{0:T(128)} %count_in.1, bf16[8,128,2,1024]{3,2,1,0:T(2,128)(2,1)} %bitcast.2), custom_call_target="tpu_custom_call" | custom-call | tf_op jit(solution)/shard_map/pallas_call | solution.py:316
  59.8 1.6 %copy.7 = f32[1,24,16,128]{3,2,1,0:T(8,128)} copy(f32[1,24,16,128]{3,2,1,0:T(8,128)} %bitcast.3) | data formatting | bytes 393216

commit v5 on v4

--- a/solution.py
+++ b/solution.py
@@ -170,11 +170,21 @@
     for a in range(1, per):
         for e in range(a):
             put(product(own(e), own(a)), a * (a - 1) // 2 + e)
+    landed = [0]
+
+    def pump(upto):
+        for i in range(landed[0], upto):
+            pending[i].wait_recv()
+            if i + CUT < len(pending):
+                pending[i + CUT].start()
+        landed[0] = max(landed[0], upto)
+
     lo, hi = 0, per * (per - 1) // 2
     waiting = [(reduce(0, lo, hi), lo, hi)]
     step = 1
     give = None
     if split:
+        pump(2)
         base = total.shape[0] - (per - 1)
         for e in range(per - 1):
             put(product(sent[e], spare[...]), base + e)
@@ -195,10 +205,7 @@
         base = a * (a - 1) // 2
         if split and a == nb * per - 1:
             break
-        for i in range(k * CUT, (k + 1) * CUT):
-            pending[i].wait_recv()
-            if i + CUT < len(pending):
-                pending[i + CUT].start()
+        pump((k + 1) * CUT)
 
         @pl.when(wrap == 0)
         def _():
@@ -228,8 +235,7 @@
     if split:
         half = BLK // 2
         for h in range(2):
-            for i in range(k * CUT + 2 * h, k * CUT + 2 * h + 2):
-                pending[i].wait_recv()
+            pump(k * CUT + 2 * h + 2)
             at = slice(h * half, (h + 1) * half)
 
             @pl.when(wrap == 0)

time: 61.5 us -> 61.5 us (level)
  no operation moved by 1% of the time
where the time goes in v5:
time: 61.5 us; the launch traced here: 61.4 us
  Pallas kernels  59.8 us (97%)
  local copies, waits for them, and re-layouts  1.62 us (3%)
    pallas_call x1, Pallas kernels, shards(): pl.pallas_call(functools.partial(kernel, nb, nz, nc, per, split), out_sha...  59.8 us
    unnamed x1, local copies, waits for them, and re-layouts  1.62 us

profile of v5, /device:TPU:0, one launch (start us, length us, event | category | flops | bytes accessed | tf_op | source)
XLA Modules:
  0.0 61.4 jit_solution(1160430132512634593)
XLA Ops:
  0.0 59.8 %shard_map.55 = f32[24,16,128]{2,1,0:T(8,128)} custom-call(s32[2,8]{1,0:T(2,128)} %need_in.1, s32[2,24]{1,0:T(2,128)} %first_in.1, s32[2,24]{1,0:T(2,128)} %second_in.1, s32[2]{0:T(128)} %count_in.1, bf16[8,128,2,1024]{3,2,1,0:T(2,128)(2,1)} %bitcast.2), custom_call_target="tpu_custom_call" | custom-call | tf_op jit(solution)/shard_map/pallas_call | solution.py:322
  59.8 1.6 %copy.7 = f32[1,24,16,128]{3,2,1,0:T(8,128)} copy(f32[1,24,16,128]{3,2,1,0:T(8,128)} %bitcast.3) | data formatting | bytes 393216
